TPU v7x, 512 devices: a whole 4x8x8 slice. The times are simulated.
512 devices in a mesh: chan: 128 (over z, y, core), tm: 4 (over x).
Axes of the slice: x: 4, y: 8, z: 8, core: 2. Of those that a mesh axis runs over, the one named last changes fastest.
Arguments:
- voltage: bfloat16 [512, 64, 7168], P('chan', 'tm'), may hold values from -8 to 8
- fir_taps: float32 [12, 16], replicated, may hold values from -1.75 to 1.75
- zoom_width: int32 [224], replicated, may hold values from 1 to 16, 1792 in all
- zoom_shift: int32 [224], replicated, may hold values from 0 to 15
- owner_slot: int32 [1792], replicated, may hold values from 0 to 1791, each once
Outputs:
- fine_spectra: bfloat16 [1792, 64, 2, 512], P('chan', 'tm')
- visibility: bfloat16 [1792, 2, 512, 512], P('chan', None, 'tm')
Inputs may be any that keep to these rules, and one draw needn't show every extreme that they name: `zoom_width`: the widths sum to 1792. `owner_slot`: every position occurs once.
All inputs are finite; a program needn't handle non-finite values.
Results may differ from a plain program's by a relative error of at most 0.0033.
Values may be sent and summed in bfloat16 or wider, within the bound.
No kernel may reach another device: no remote copies, remote signals or barrier semaphores. Data moves between devices by JAX's collectives and lax.ppermute only.
A program may use at most 64 MiB of HBM per device.

v0:
```python
import functools
import math

import jax
import jax.numpy as jnp
from jax import lax
from jax.experimental import pallas as pl
from jax.experimental.pallas import tpu as pltpu
from jax.sharding import PartitionSpec as P

VMEM = pltpu.VMEM
BF16 = jnp.bfloat16
F32 = jnp.float32
LIMIT = 32 * 1024 * 1024
MOST = 64 * 1000 * 1000
WIDE = 272


def dft_weights(phases, coarse):
    shape = (2 * phases, 2 * phases * coarse)
    source = lax.broadcasted_iota(jnp.int32, shape, 0)
    target = lax.broadcasted_iota(jnp.int32, shape, 1)
    j, p = source % phases, source // phases
    b, d, q = target % phases, (target // phases) % coarse, target // (phases * coarse)
    turn = (j * b + jnp.where(p == q, 0, jnp.where(q == 0, 3, 1) * phases // 4)) % phases
    table = jnp.zeros(shape, F32)
    for k in range(phases):
        exact = round(math.cos(2.0 * math.pi * k / phases), 15) / math.sqrt(phases)
        table = jnp.where(turn == k, jnp.float32(exact), table)
    return split_sum(jnp.concatenate([jnp.where(d == c, table, 0.0) for c in range(coarse)], 0))


def spread_taps(taps):
    phases = taps.shape[1]
    wide = jnp.concatenate([taps, jnp.zeros((taps.shape[0], 128 - phases), F32)], 1)
    while phases < 128:
        wide = wide + pltpu.roll(wide, phases, 1)
        phases *= 2
    return wide


def tap_tables(taps):
    row = lax.broadcasted_iota(jnp.int32, (8, 128), 0)
    tap = [jnp.broadcast_to(taps[m : m + 1, :], (8, 128)) for m in range(taps.shape[0])]
    zero = jnp.zeros((8, 128), F32)
    same = [jnp.where(row >= k, tap[k], zero) for k in range(1, 8)]
    beyond = [jnp.where(row < k, tap[8 + k], zero) for k in range(1, 4)]
    before = [jnp.where(row < k, tap[k], tap[8 + k] if k < 4 else zero) for k in range(1, 8)]
    return tap[0], tap[8], same, before, beyond


def split_sum(value):
    high = value.astype(BF16)
    return high, (value - high.astype(F32)).astype(BF16)


def fetch(sems, *pairs):
    copies = [
        pltpu.make_async_copy(source, target, sems.at[i]) for i, (source, target) in enumerate(pairs)
    ]
    for copy in copies:
        copy.start()
    return copies


def window_table(krow):
    shape = (WIDE, krow.shape[1])
    row = lax.broadcasted_iota(jnp.int32, shape, 0).astype(jnp.int16)
    column = jnp.broadcast_to(krow, shape).astype(jnp.int16)
    return jnp.where(row == column, jnp.ones(shape, BF16), jnp.zeros(shape, BF16))


def store_windows(window_ref, base, picked, step):
    base = pl.multiple_of(base, 16)
    lanes = slice(0, picked.shape[1])
    if step > 0:
        meet = pl.ds(base, 16)
        window_ref[meet, lanes] = window_ref[meet, lanes] + picked[:16]
        window_ref[pl.ds(pl.multiple_of(base + 16, 16), WIDE - 16), lanes] = picked[16:]
    else:
        window_ref[0:WIDE, lanes] = picked


def tail_kernel(
    width_from, shift_from, voltage_ref, taps_from,
    out_ref, rest_ref, base_ref,
    width_ref, shift_ref, taps_ref, held_ref, member_ref, split_high_ref, split_low_ref, table_ref, window_ref, sems,
):
    inputs, _, samples = held_ref.shape
    fine = window_ref.shape[0] - 256
    lanes = 128
    phases = 16
    copies = fetch(
        sems,
        (width_from, width_ref),
        (shift_from, shift_ref),
        (taps_from, taps_ref),
        (voltage_ref, held_ref),
    )
    high_table, low_table = dft_weights(phases, 8)
    weights = jnp.concatenate([high_table, high_table, low_table], 0)
    copies[0].wait()
    copies[1].wait()
    lane = lax.broadcasted_iota(jnp.int32, (1, lanes), 1)
    place = lane // phases
    bins = lane % phases
    first = jnp.int32(0)
    bases = []
    for step in range(samples // 512):
        base = (first // 16) * 16
        base_ref[step] = base
        bases.append(base)
        rows = []
        for half in range(2):
            width = jnp.zeros((1, lanes), jnp.int32)
            shift = jnp.zeros((1, lanes), jnp.int32)
            begin = jnp.zeros((1, lanes), jnp.int32)
            for c in range(8):
                at = step * 16 + half * 8 + c
                here = place == c
                wide = width_ref[at]
                width = jnp.where(here, wide, width)
                shift = jnp.where(here, shift_ref[at], shift)
                begin = jnp.where(here, first, begin)
                first = first + wide
            room = (phases + 1 - width).astype(F32)
            whole = jnp.floor((shift.astype(F32) + 0.5) / room)
            start = shift - (whole * room).astype(jnp.int32)
            offset = bins - start
            inside = (offset >= 0) & (offset < width)
            rows.append(jnp.where(inside, begin + offset, -1))
        krow = jnp.concatenate(rows, 1) - base
        rest_ref[step : step + 1, :] = krow.astype(F32)
        member_ref[step * WIDE : (step + 1) * WIDE, :] = window_table(krow)

    copies[2].wait()
    taps = spread_taps(taps_ref[...])
    rest_ref[16 : 16 + taps.shape[0], 0:lanes] = taps
    _, eighth, _, before, beyond = tap_tables(taps)
    window_ref[:, 96:lanes] = jnp.zeros((window_ref.shape[0], lanes - 96), F32)
    copies[3].wait()

    def group(step, carry):
        for sub in range(2):
            spot = pl.ds(pl.multiple_of(step * 256 + sub * lanes, lanes), lanes)
            tops, bottoms = [], []
            for i in range(inputs):
                series = held_ref[i, :, spot].astype(F32)
                older, recent = series[:8], series[8:]
                top = eighth * recent
                bottom = jnp.zeros((8, lanes), F32)
                for k in range(1, 8):
                    recent_k = pltpu.roll(recent, k, 0)
                    top = top + before[k - 1] * recent_k
                    if k < 4:
                        top = top + beyond[k - 1] * pltpu.roll(older, k, 0)
                        bottom = bottom + beyond[k - 1] * recent_k
                tops.append(top)
                bottoms.append(bottom if i % 2 == 0 else pltpu.roll(bottom, 4, 0))
            packed = [bottoms[i] + bottoms[i + 1] for i in range(0, inputs, 2)]
            high, low = split_sum(jnp.concatenate(tops + packed, 0))
            at = pl.ds(pl.multiple_of(step * 48, 16), 48)
            split_high_ref[at, sub * lanes : (sub + 1) * lanes] = high
            split_low_ref[at, sub * lanes : (sub + 1) * lanes] = low
        return carry

    lax.fori_loop(0, samples // 256, group, 0)
    for step in range(samples // 1024):
        at = slice(step * 192, step * 192 + 192)
        high = split_high_ref[at, :]
        split = jnp.concatenate([high, split_low_ref[at, :], high], 1)
        spectra = jnp.dot(split, weights, preferred_element_type=F32).astype(BF16)
        for j in range(4):
            for q in range(2):
                to = (step * 2 + j // 2) * 96
                half = slice((j % 2) * lanes, (j % 2 + 1) * lanes)
                piece = spectra[j * 48 : (j + 1) * 48, q * lanes : (q + 1) * lanes]
                table_ref[to + q * 32 : to + q * 32 + 32, half] = piece[:32]
                table_ref[to + 64 + q * 16 : to + 64 + q * 16 + 16, half] = piece[32:]
    for step in range(samples // 512):
        picked = lax.dot_general(
            member_ref[step * WIDE : (step + 1) * WIDE, :],
            table_ref[step * 96 : (step + 1) * 96, :],
            (((1,), (1,)), ((), ())),
            preferred_element_type=F32,
        )
        store_windows(window_ref, bases[step], picked, step)
    half, quarter = fine // 2, fine // 4
    at = lax.broadcasted_iota(jnp.int32, (half, lanes), 1)
    out_ref[0:half, :] = jnp.where(
        at < 64, window_ref[0:half, :], pltpu.roll(window_ref[half:fine, :], 64, 1)
    ).astype(BF16)
    at = lax.broadcasted_iota(jnp.int32, (quarter, lanes), 1)
    packed = jnp.zeros((quarter, lanes), F32)
    for j in range(4):
        moved = pltpu.roll(window_ref[j * quarter : (j + 1) * quarter, :], (64 + j * 32) % lanes, 1)
        packed = jnp.where(at // 32 == j, moved, packed)
    out_ref[half : half + quarter, :] = packed.astype(BF16)


def own_kernel(
    base_from, voltage_ref, rest_from,
    window_ref,
    base_ref, rest_ref, held_ref, split_high_ref, split_low_ref, table_ref, sems,
):
    inputs, blocks, samples = held_ref.shape
    lanes = 128
    copies = fetch(sems, (rest_from, rest_ref), (base_from, base_ref), (voltage_ref, held_ref))
    high_table, low_table = dft_weights(16, 8)
    weights = jnp.concatenate([high_table, high_table, low_table], 0)
    for copy in copies:
        copy.wait()
    first, eighth, same, before, _ = tap_tables(rest_ref[16:28, 0:lanes])

    def group(step, carry):
        for i in range(inputs):
            for sub in range(2):
                spot = pl.ds(pl.multiple_of(step * 256 + sub * lanes, lanes), lanes)
                series = held_ref[i, :, spot].astype(F32)
                early, late = series[:8], series[8:]
                top = first * early
                bottom = first * late + eighth * early
                for k in range(1, 8):
                    early_k = pltpu.roll(early, k, 0)
                    top = top + same[k - 1] * early_k
                    bottom = bottom + before[k - 1] * early_k
                    bottom = bottom + same[k - 1] * pltpu.roll(late, k, 0)
                at = pl.ds(pl.multiple_of(step * 64 + i * blocks, blocks), blocks)
                high, low = split_sum(jnp.concatenate([top, bottom], 0))
                split_high_ref[at, sub * lanes : (sub + 1) * lanes] = high
                split_low_ref[at, sub * lanes : (sub + 1) * lanes] = low
        return carry

    lax.fori_loop(0, samples // 256, group, 0)
    for step in range(samples // 1024):
        at = slice(step * 256, step * 256 + 256)
        high = split_high_ref[at, :]
        split = jnp.concatenate([high, split_low_ref[at, :], high], 1)
        parts = split_sum(jnp.dot(split, weights, preferred_element_type=F32))
        for j in range(4):
            for q in range(2):
                for p in range(2):
                    to = (step * 2 + j // 2) * 256 + p * 128 + q * 64
                    table_ref[to : to + 64, (j % 2) * 128 : (j % 2) * 128 + 128] = parts[p][
                        j * 64 : (j + 1) * 64, q * 128 : (q + 1) * 128
                    ]
    for step in range(samples // 512):
        picked = lax.dot_general(
            window_table(rest_ref[step : step + 1, :].astype(jnp.int32)),
            table_ref[step * 256 : (step + 1) * 256, :],
            (((1,), (1,)), ((), ())),
            preferred_element_type=F32,
        )
        store_windows(window_ref, base_ref[step], picked[:, :lanes] + picked[:, lanes:], step)


def place_kernel(slot_ref, place_ref):
    fine = slot_ref.shape[1]
    rows = 16
    row = lax.broadcasted_iota(jnp.int32, (rows, fine), 0)
    slot = jnp.broadcast_to(slot_ref[...], (rows, fine))
    row, slot = row.astype(jnp.int16), slot.astype(jnp.int16)
    one, zero = jnp.ones((rows, fine), BF16), jnp.zeros((rows, fine), BF16)

    def places(step, carry):
        at = pl.multiple_of(step * rows, rows)
        here = row + at.astype(jnp.int16)
        place_ref[pl.ds(at, rows), :] = jnp.where(here == slot, one, zero)
        return carry

    lax.fori_loop(0, place_ref.shape[0] // rows, places, 0, unroll=4)


def send_kernel(window_ref, tail_ref, place_ref, out_ref, bins_ref):
    fine, lanes = bins_ref.shape
    half, quarter = fine // 2, fine // 4
    source = lax.broadcasted_iota(jnp.int32, (lanes, lanes), 0)
    target = lax.broadcasted_iota(jnp.int32, (lanes, lanes), 1)
    late = source - 64
    early_lane = (source // 8) * 16 + source % 8
    late_lane = (late // 4) * 16 + 8 + late % 4
    spread = jnp.where(
        ((source < 64) & (target == early_lane))
        | ((source >= 64) & (source < 96) & (late % 4 < 3) & (target == late_lane)),
        1.0,
        0.0,
    ).astype(BF16)
    at = lax.broadcasted_iota(jnp.int32, (quarter, lanes), 1)
    for j in range(4):
        rows = slice((j % 2) * quarter, (j % 2 + 1) * quarter)
        early = tail_ref[rows, :].astype(F32)
        if j >= 2:
            early = pltpu.roll(early, 64, 1)
        late = tail_ref[half : half + quarter, :].astype(F32)
        late = pltpu.roll(late, (64 - j * 32) % lanes, 1)
        tail = jnp.where(at < 64, early, late).astype(BF16)
        added = jnp.dot(tail, spread, preferred_element_type=F32)
        rows = slice(j * quarter, (j + 1) * quarter)
        bins_ref[rows, :] = (window_ref[rows, :] + added).astype(BF16)
    step_rows = 448
    for step in range(out_ref.shape[0] // step_rows):
        at = slice(step * step_rows, (step + 1) * step_rows)
        out_ref[at, :] = jnp.dot(
            place_ref[at, :], bins_ref[...], preferred_element_type=F32
        ).astype(BF16)


def unpack_kernel(received_ref, out_ref, wide_ref, *, inputs_dev):
    fine_dev = out_ref.shape[0]
    rows, lanes = received_ref.shape
    devices = rows // fine_dev
    blocks = lanes // (2 * inputs_dev)
    wide_ref[...] = received_ref[...].astype(F32)
    inputs = inputs_dev * devices
    source = lax.broadcasted_iota(jnp.int32, (inputs, inputs), 0)
    target = lax.broadcasted_iota(jnp.int32, (inputs, inputs), 1)
    spread = jnp.where((source % devices) * inputs_dev + source // devices == target, 1.0, 0.0)
    spread = spread.astype(BF16)
    pieces = []
    for channel in range(fine_dev):
        turned = wide_ref[pl.ds(channel, devices, stride=fine_dev), :].T.astype(BF16)
        for q in range(2):
            pieces.append(
                jnp.concatenate(
                    [
                        turned[(q * inputs_dev + i) * blocks : (q * inputs_dev + i + 1) * blocks, :]
                        for i in range(inputs_dev)
                    ],
                    1,
                )
            )
    joined = jnp.concatenate(pieces, 0)
    placed = jnp.dot(joined, spread, preferred_element_type=F32).astype(BF16)
    out_ref[...] = placed.reshape(out_ref.shape)


def correlate_kernel(mine_ref, own_ref, ahead_ref, behind_ref, across_ref, *rest, scale, first):
    out_ref, block_ref, sems = rest[-3:]
    mine = pl.ds(pl.multiple_of(mine_ref[0], 128), 128)
    half = own_ref.shape[1] // 2
    copies = []
    for channel in range(across_ref.shape[0]):
        refs = [ref.at[first + channel] for ref in (own_ref, ahead_ref, behind_ref)]
        refs.append(across_ref.at[channel])
        right = jnp.concatenate([ref[...] for ref in refs], 0)
        real, imag = [], []
        for ref in refs:
            block = ref[:, mine]
            real.append(block)
            imag.append(block[half:])
            imag.append(-block[:half])
        left = jnp.concatenate([jnp.concatenate(real, 0), jnp.concatenate(imag, 0)], 1)
        product = lax.dot_general(
            left, right, (((0,), (0,)), ((), ())), preferred_element_type=F32
        )
        product = (product * scale).astype(BF16)
        block_ref[channel, 0] = product[:128]
        block_ref[channel, 1] = product[128:]
        copies.append(
            pltpu.make_async_copy(
                block_ref.at[channel], out_ref.at[first + channel], sems.at[channel]
            )
        )
        copies[-1].start()
    for copy in copies:
        copy.wait()


WHOLE = pl.BlockSpec(memory_space=VMEM)
SCALARS = pl.BlockSpec(memory_space=pltpu.SMEM)
APART = pl.BlockSpec(memory_space=pl.ANY)


def tail_part(voltage, fir_taps, zoom_width, zoom_shift, fine):
    inputs_dev, blocks, samples = voltage.shape
    groups = samples // 256
    return pl.pallas_call(
        tail_kernel,
        out_shape=(
            jax.ShapeDtypeStruct((fine // 2 + fine // 4, 128), BF16),
            jax.ShapeDtypeStruct((32, 256), F32),
            jax.ShapeDtypeStruct((samples // 512,), jnp.int32),
        ),
        in_specs=[APART] * 4,
        out_specs=(WHOLE, WHOLE, SCALARS),
        scratch_shapes=[
            pltpu.SMEM(zoom_width.shape, jnp.int32),
            pltpu.SMEM(zoom_shift.shape, jnp.int32),
            pltpu.VMEM(fir_taps.shape, F32),
            pltpu.VMEM(voltage.shape, BF16),
            pltpu.VMEM((samples // 512 * WIDE, 256), BF16),
            pltpu.VMEM((groups * 48, 256), BF16),
            pltpu.VMEM((groups * 48, 256), BF16),
            pltpu.VMEM((groups * 48, 256), BF16),
            pltpu.VMEM((fine + 256, 128), F32),
            pltpu.SemaphoreType.DMA((4,)),
        ],
        compiler_params=pltpu.CompilerParams(vmem_limit_bytes=MOST),
        name="tail_part",
    )(zoom_width, zoom_shift, voltage, fir_taps)


def own_part(voltage, rest, base, fine):
    inputs_dev, blocks, samples = voltage.shape
    groups = samples // 256
    return pl.pallas_call(
        own_kernel,
        out_shape=jax.ShapeDtypeStruct((fine + 256, 128), F32),
        in_specs=[APART] * 3,
        out_specs=WHOLE,
        scratch_shapes=[
            pltpu.SMEM(base.shape, jnp.int32),
            pltpu.VMEM(rest.shape, F32),
            pltpu.VMEM(voltage.shape, BF16),
            pltpu.VMEM((groups * 64, 256), BF16),
            pltpu.VMEM((groups * 64, 256), BF16),
            pltpu.VMEM((groups * 128, 256), BF16),
            pltpu.SemaphoreType.DMA((3,)),
        ],
        compiler_params=pltpu.CompilerParams(vmem_limit_bytes=MOST),
        cost_estimate=pl.CostEstimate(flops=5_000_000_000, bytes_accessed=4_000_000, transcendentals=0),
        name="own_part",
    )(base, voltage, rest)


def place_part(slot):
    fine = slot.shape[1]
    return pl.pallas_call(
        place_kernel,
        out_shape=jax.ShapeDtypeStruct((fine, fine), BF16),
        in_specs=[WHOLE],
        out_specs=WHOLE,
        compiler_params=pltpu.CompilerParams(vmem_limit_bytes=LIMIT),
        cost_estimate=pl.CostEstimate(flops=5_000_000_000, bytes_accessed=4_000_000, transcendentals=0),
        name="place_part",
    )(slot)


def send_part(window, tail, place):
    slots, fine = place.shape
    return pl.pallas_call(
        send_kernel,
        out_shape=jax.ShapeDtypeStruct((slots, 128), BF16),
        in_specs=[WHOLE] * 3,
        out_specs=WHOLE,
        scratch_shapes=[pltpu.VMEM((fine, 128), BF16)],
        compiler_params=pltpu.CompilerParams(vmem_limit_bytes=LIMIT),
        name="send_part",
    )(window, tail, place)


def unpack(received, fine_dev, inputs_dev):
    rows, lanes = received.shape
    devices = rows // fine_dev
    blocks = lanes // (2 * inputs_dev)
    whole = pl.BlockSpec(memory_space=VMEM)
    return pl.pallas_call(
        functools.partial(unpack_kernel, inputs_dev=inputs_dev),
        out_shape=jax.ShapeDtypeStruct((fine_dev, 2 * blocks, devices * inputs_dev), BF16),
        in_specs=[whole],
        out_specs=whole,
        scratch_shapes=[pltpu.VMEM((rows, lanes), F32)],
        compiler_params=pltpu.CompilerParams(vmem_limit_bytes=LIMIT),
        name="unpack",
    )(received)


def correlate(near, across, mine, scale, first, earlier=None):
    fine_dev, rows, inputs = near[0].shape
    fine_part = across.shape[0]
    whole = pl.BlockSpec(memory_space=VMEM)
    apart = pl.BlockSpec(memory_space=pl.ANY)
    held = [] if earlier is None else [earlier]
    return pl.pallas_call(
        functools.partial(correlate_kernel, scale=scale, first=first),
        out_shape=jax.ShapeDtypeStruct((fine_dev, 2, 128, inputs), BF16),
        in_specs=[pl.BlockSpec(memory_space=pltpu.SMEM)] + [whole] * 4 + [apart] * len(held),
        out_specs=apart,
        scratch_shapes=[
            pltpu.VMEM((fine_part, 2, 128, inputs), BF16),
            pltpu.SemaphoreType.DMA((fine_part,)),
        ],
        input_output_aliases={5: 0} if held else {},
        compiler_params=pltpu.CompilerParams(vmem_limit_bytes=LIMIT),
        cost_estimate=pl.CostEstimate(
            flops=2 * fine_part * 256 * inputs * 4 * rows,
            bytes_accessed=4_000_000,
            transcendentals=0,
        ),
        name="correlate",
    )(mine, *near, across, *held)


def local(voltage, fir_taps, zoom_width, zoom_shift, owner_slot):
    inputs_dev, blocks, samples = voltage.shape
    devices = lax.axis_size("chan")
    groups = lax.axis_size("tm")
    fine = owner_slot.shape[0]
    fine_dev = fine // devices
    up = [(i, i + 1) for i in range(groups - 1)]
    tail, rest, base = tail_part(voltage, fir_taps, zoom_width, zoom_shift, fine)
    tail = lax.ppermute(tail, "tm", up)
    window = own_part(voltage, rest, base, fine)
    slot, window = lax.optimization_barrier((owner_slot, window))
    place = place_part(slot[None, :])
    sent = send_part(window, tail, place)
    lanes = sent.shape[1]
    received = lax.all_to_all(
        sent.reshape(devices, fine_dev // 2, 2, lanes), "chan", split_axis=0, concat_axis=0, tiled=True
    )
    own = unpack(received.reshape(fine, lanes), fine_dev, inputs_dev)

    def around(turn):
        pairs = []
        for c in range(devices):
            for g in range(groups):
                to = (g + (turn if c % 2 == 0 else -turn)) % groups
                pairs.append((c * groups + g, c * groups + to))
        return pairs

    both = ("chan", "tm")
    ahead = lax.ppermute(own, both, around(1))
    spectra = jnp.transpose(own.reshape(fine_dev, 2, blocks, own.shape[2]), (0, 2, 1, 3))
    later, spectra = lax.optimization_barrier((own, spectra))
    behind = lax.ppermute(later, both, around(-1))
    first = fine_dev * 8 // 14
    across_a = lax.ppermute(ahead[:first], both, around(1))
    across_b = lax.ppermute(ahead[first:], both, around(1))
    mine = (lax.axis_index("tm") * 128).astype(jnp.int32)[None]
    scale = 1.0 / (blocks * groups)
    near = (own, ahead, behind)
    summed = correlate(near, across_a, mine, scale, 0)
    summed = correlate(near, across_b, mine, scale, first, summed)
    return spectra, summed


def solution(mesh):
    return jax.shard_map(
        local,
        mesh=mesh,
        in_specs=(P("chan", "tm", None), P(), P(), P(), P()),
        out_specs=(P("chan", "tm", None, None), P("chan", None, "tm", None)),
        check_vma=False,
    )
```

profile of v0, /device:TPU:1, one launch (start us, length us, event | category | flops | bytes accessed | tf_op | source)
XLA Modules:
  0.0 82.3 jit_solution(17988691560646724269)
XLA Ops:
  0.6 5.3 %tail_part.1 = (bf16[1344,128]{1,0:T(8,128)(2,1)}, f32[32,256]{1,0:T(8,128)}, s32[14]{0:T(128)}) custom-call(s32[224]{0:T(256)} %width_from.1, s32[224]{0:T(256)} %shift_from.1, bf16[4,16,7168]{2,1,0:T(8,128)(2,1)} %voltage_ref.3, f32[12,16]{1,0:T(8,128)} %taps_from.1), custom_call_target="tpu_custom_call" | custom-call | tf_op jit(solution)/shard_map/tail_part/pallas_call | solution.py:377
  5.9 4.0 %collective-permute-start = (bf16[1344,128]{1,0:T(8,128)(2,1)}, bf16[1344,128]{1,0:T(8,128)(2,1)S(1)}, u32[]{:S(2)}, u32[]{:S(2)}) collective-permute-start(bf16[1344,128]{1,0:T(8,128)(2,1)} %get-tuple-element.12), channel_id=1, source_target_pairs={{0,1},{1,2},{2,3},{4,5},{5,6},{6,7},{8,9},{9,10},{10,11},{12,13},{... | collective-permute-start | bytes 1032200 | tf_op jit(solution)/shard_map/ppermute | solution.py:502
  9.9 0.0 copy-start.1
  9.9 6.1 %own_part.1.window_ref = f32[2048,128]{1,0:T(8,128)} custom-call(s32[14]{0:T(128)} %get-tuple-element.9.base_from, bf16[4,16,7168]{2,1,0:T(8,128)(2,1)} %voltage_ref.3, f32[32,256]{1,0:T(8,128)} %get-tuple-element.10.rest_from), custom_call_target="tpu_custom_call" | custom-call | flops 5000000000 | bytes 4000000 | tf_op jit(solution)/shard_map/own_part/pallas_call | solution.py:406
  15.9 0.0 copy-done.1
  16.0 0.0 copy-start
  16.0 0.9 %place_part.1.place_ref = bf16[1792,1792]{1,0:T(8,128)(2,1)S(1)} custom-call(s32[1,1792]{1,0:T(1,128)S(1)} %broadcast_in_dim.6.slot_ref), custom_call_target="tpu_custom_call" | custom-call | flops 5000000000 | bytes 4000000 | tf_op jit(solution)/shard_map/place_part/pallas_call | solution.py:428
  16.9 0.0 collective-permute-done.tail_ref
  16.9 0.3 copy-done
  17.2 2.0 %send_part.1 = bf16[1792,128]{1,0:T(8,128)(2,1)S(1)} custom-call(f32[2048,128]{1,0:T(8,128)S(1)} %copy-done, bf16[1344,128]{1,0:T(8,128)(2,1)S(1)} %collective-permute-done.tail_ref, bf16[1792,1792]{1,0:T(8,128)(2,1)S(1)} %place_part.1.place_ref), custom_call_target="tpu_custom_call" | custom-call | tf_op jit(solution)/shard_map/send_part/pallas_call | solution.py:441
  19.2 37.2 %all_to_all.5 = bf16[128,7,2,128]{3,2,1,0:T(2,128)(2,1)S(1)} all-to-all(bf16[128,7,2,128]{3,2,1,0:T(2,128)(2,1)S(1)} %bitcast.9), channel_id=1, replica_groups=mesh['chan'=128,'tm'=4] {'chan'}, dimensions={0} | all-to-all | bytes 917504 | tf_op jit(solution)/shard_map/all_to_all | solution.py:508
  56.4 0.5 unpack.1.own_ref
  56.9 5.3 %collective-permute-start.1 = (bf16[14,32,512]{2,1,0:T(8,128)(2,1)S(1)}, bf16[14,32,512]{2,1,0:T(8,128)(2,1)S(1)}, u32[]{:S(2)}, u32[]{:S(2)}) collective-permute-start(bf16[14,32,512]{2,1,0:T(8,128)(2,1)S(1)} %unpack.1.own_ref), channel_id=1, source_target_pairs={{0,1},{1,2},{2,3},{3,0},{4,7},{5,4},{6,5},{7,6},{8,9},{9,10},{10,1... | collective-permute-start | bytes 1376264 | tf_op jit(solution)/shard_map/ppermute | solution.py:522
  62.2 1.2 %copy.10 = bf16[14,2,16,512]{3,1,2,0:T(2,128)(2,1)} copy(bf16[14,2,16,512]{3,2,1,0:T(8,128)(2,1)S(1)} %bitcast.7) | data formatting | bytes 917504 | tf_op jit(solution)/shard_map/reshape | solution.py:523
  63.5 1.9 %collective-permute-start.2 = (bf16[14,32,512]{2,1,0:T(8,128)(2,1)S(1)}, bf16[14,32,512]{2,1,0:T(8,128)(2,1)S(1)}, u32[]{:S(2)}, u32[]{:S(2)}) collective-permute-start(bf16[14,32,512]{2,1,0:T(8,128)(2,1)S(1)} %unpack.1.own_ref), channel_id=1, source_target_pairs={{0,3},{1,0},{2,1},{3,2},{4,5},{5,6},{6,7},{7,4},{8,11},{9,8},{10,9... | collective-permute-start | bytes 1376264 | tf_op jit(solution)/shard_map/ppermute | solution.py:525
  65.4 3.5 %collective-permute-done.1.ahead_ref = bf16[14,32,512]{2,1,0:T(8,128)(2,1)S(1)} collective-permute-done((bf16[14,32,512]{2,1,0:T(8,128)(2,1)S(1)}, bf16[14,32,512]{2,1,0:T(8,128)(2,1)S(1)}, u32[]{:S(2)}, u32[]{:S(2)}) %collective-permute-start.1) | collective-permute-done | bytes 458784 | tf_op jit(solution)/shard_map/ppermute | solution.py:522
  68.9 5.3 %collective-permute-start.4 = (bf16[8,32,512]{2,1,0:T(8,128)(2,1)S(1)}, bf16[8,32,512]{2,1,0:T(8,128)(2,1)S(1)}, u32[]{:S(2)}, u32[]{:S(2)}) collective-permute-start(bf16[8,32,512]{2,1,0:T(8,128)(2,1)S(1)} %slice.9), channel_id=1, source_target_pairs={{0,1},{1,2},{2,3},{3,0},{4,7},{5,4},{6,5},{7,6},{8,9},{9,10},{10,1... | collective-permute-start | bytes 786440 | tf_op jit(solution)/shard_map/ppermute | solution.py:527
  74.3 1.9 %collective-permute-start.3 = (bf16[6,32,512]{2,1,0:T(8,128)(2,1)S(1)}, bf16[6,32,512]{2,1,0:T(8,128)(2,1)S(1)}, u32[]{:S(2)}, u32[]{:S(2)}) collective-permute-start(bf16[6,32,512]{2,1,0:T(8,128)(2,1)S(1)} %slice.8), channel_id=1, source_target_pairs={{0,1},{1,2},{2,3},{3,0},{4,7},{5,4},{6,5},{7,6},{8,9},{9,10},{10,1... | collective-permute-start | bytes 589832 | tf_op jit(solution)/shard_map/ppermute | solution.py:528
  76.2 0.0 collective-permute-done.2.behind_ref
  76.2 1.3 %collective-permute-done.4.across_ref = bf16[8,32,512]{2,1,0:T(8,128)(2,1)S(1)} collective-permute-done((bf16[8,32,512]{2,1,0:T(8,128)(2,1)S(1)}, bf16[8,32,512]{2,1,0:T(8,128)(2,1)S(1)}, u32[]{:S(2)}, u32[]{:S(2)}) %collective-permute-start.4) | collective-permute-done | bytes 262176 | tf_op jit(solution)/shard_map/ppermute | solution.py:527
  77.6 1.6 %correlate.2.rest_0_ = bf16[14,2,128,512]{3,2,1,0:T(8,128)(2,1)} custom-call(s32[1]{0:T(128)} %bitcast.4.mine_ref, bf16[14,32,512]{2,1,0:T(8,128)(2,1)S(1)} %unpack.1.own_ref, bf16[14,32,512]{2,1,0:T(8,128)(2,1)S(1)} %collective-permute-done.1.ahead_ref, bf16[14,32,512]{2,1,0:T(8,128)(2,1)S(1)} %collective-permute-done.2.behind_ref, ...), custom_call_target="tpu_custom_call" | custom-call | flops 268435456 | bytes 4000000 | tf_op jit(solution)/shard_map/correlate/pallas_call | solution.py:474
  79.2 1.7 %collective-permute-done.3.across_ref = bf16[6,32,512]{2,1,0:T(8,128)(2,1)S(1)} collective-permute-done((bf16[6,32,512]{2,1,0:T(8,128)(2,1)S(1)}, bf16[6,32,512]{2,1,0:T(8,128)(2,1)S(1)}, u32[]{:S(2)}, u32[]{:S(2)}) %collective-permute-start.3) | collective-permute-done | bytes 196640 | tf_op jit(solution)/shard_map/ppermute | solution.py:528
  80.9 1.4 %correlate.3 = bf16[14,2,128,512]{3,2,1,0:T(8,128)(2,1)} custom-call(s32[1]{0:T(128)} %bitcast.4.mine_ref, bf16[14,32,512]{2,1,0:T(8,128)(2,1)S(1)} %unpack.1.own_ref, bf16[14,32,512]{2,1,0:T(8,128)(2,1)S(1)} %collective-permute-done.1.ahead_ref, bf16[14,32,512]{2,1,0:T(8,128)(2,1)S(1)} %collective-permute-done.2.behind_ref, ...), custom_call_target="tpu_custom_call", output_to_operand_aliasing={{}: (5, {})} | custom-call | flops 201326592 | bytes 4000000 | tf_op jit(solution)/shard_map/correlate/pallas_call | solution.py:474
  (3 shorter events, 0.0 us)
Async XLA Ops:
  5.9 11.0 %collective-permute-start = (bf16[1344,128]{1,0:T(8,128)(2,1)}, bf16[1344,128]{1,0:T(8,128)(2,1)S(1)}, u32[]{:S(2)}, u32[]{:S(2)}) collective-permute-start(bf16[1344,128]{1,0:T(8,128)(2,1)} %get-tuple-element.12), channel_id=1, source_target_pairs={{0,1},{1,2},{2,3},{4,5},{5,6},{6,7},{8,9},{9,10},{10,11},{12,13},{... | collective-permute-start | bytes 1032200 | tf_op jit(solution)/shard_map/ppermute | solution.py:502
  9.9 6.1 %copy-start.1 = (s32[1792]{0:T(1024)S(1)}, s32[1792]{0:T(1024)}, u32[]{:S(2)}) copy-start(s32[1792]{0:T(1024)} %param.9) | copy-start | bytes 21508
  16.0 1.2 %copy-start = (f32[2048,128]{1,0:T(8,128)S(1)}, f32[2048,128]{1,0:T(8,128)}, u32[]{:S(2)}) copy-start(f32[2048,128]{1,0:T(8,128)} %own_part.1.window_ref) | copy-start | bytes 3145732
  56.9 12.0 %collective-permute-start.1 = (bf16[14,32,512]{2,1,0:T(8,128)(2,1)S(1)}, bf16[14,32,512]{2,1,0:T(8,128)(2,1)S(1)}, u32[]{:S(2)}, u32[]{:S(2)}) collective-permute-start(bf16[14,32,512]{2,1,0:T(8,128)(2,1)S(1)} %unpack.1.own_ref), channel_id=1, source_target_pairs={{0,1},{1,2},{2,3},{3,0},{4,7},{5,4},{6,5},{7,6},{8,9},{9,10},{10,1... | collective-permute-start | bytes 1376264 | tf_op jit(solution)/shard_map/ppermute | solution.py:522
  63.5 12.7 %collective-permute-start.2 = (bf16[14,32,512]{2,1,0:T(8,128)(2,1)S(1)}, bf16[14,32,512]{2,1,0:T(8,128)(2,1)S(1)}, u32[]{:S(2)}, u32[]{:S(2)}) collective-permute-start(bf16[14,32,512]{2,1,0:T(8,128)(2,1)S(1)} %unpack.1.own_ref), channel_id=1, source_target_pairs={{0,3},{1,0},{2,1},{3,2},{4,5},{5,6},{6,7},{7,4},{8,11},{9,8},{10,9... | collective-permute-start | bytes 1376264 | tf_op jit(solution)/shard_map/ppermute | solution.py:525
  68.9 8.6 %collective-permute-start.4 = (bf16[8,32,512]{2,1,0:T(8,128)(2,1)S(1)}, bf16[8,32,512]{2,1,0:T(8,128)(2,1)S(1)}, u32[]{:S(2)}, u32[]{:S(2)}) collective-permute-start(bf16[8,32,512]{2,1,0:T(8,128)(2,1)S(1)} %slice.9), channel_id=1, source_target_pairs={{0,1},{1,2},{2,3},{3,0},{4,7},{5,4},{6,5},{7,6},{8,9},{9,10},{10,1... | collective-permute-start | bytes 786440 | tf_op jit(solution)/shard_map/ppermute | solution.py:527
  74.3 6.6 %collective-permute-start.3 = (bf16[6,32,512]{2,1,0:T(8,128)(2,1)S(1)}, bf16[6,32,512]{2,1,0:T(8,128)(2,1)S(1)}, u32[]{:S(2)}, u32[]{:S(2)}) collective-permute-start(bf16[6,32,512]{2,1,0:T(8,128)(2,1)S(1)} %slice.8), channel_id=1, source_target_pairs={{0,1},{1,2},{2,3},{3,0},{4,7},{5,4},{6,5},{7,6},{8,9},{9,10},{10,1... | collective-permute-start | bytes 589832 | tf_op jit(solution)/shard_map/ppermute | solution.py:528
where the time goes:
time: 82.6 us; the launch traced here: 82.3 us
  blocking collectives  37.2 us (45%)
  starting transfers between devices  18.4 us (22%)
  Pallas kernels  17.9 us (22%)
  waiting for transfers between devices  6.53 us (8%)
  local copies, waits for them, and re-layouts  1.55 us (2%)
    all_to_all x1, blocking collectives, local(): lax.all_to_all(sent.reshape(devices, fine_dev // 2, 2, lanes), 'chan', sp...  37.2 us
    pallas_call x1, Pallas kernels, own_part(): pl.pallas_call(own_kernel, out_shape=jax.ShapeDtypeStruct((fine + 256, 12...  6.07 us
    ppermute x1, starting transfers between devices, local(): across_a = lax.ppermute(ahead[:first], both, around(1))  5.32 us
    ppermute x1, starting transfers between devices, local(): ahead = lax.ppermute(own, both, around(1))  5.28 us
    pallas_call x1, Pallas kernels, tail_part(): pl.pallas_call(tail_kernel, out_shape=(jax.ShapeDtypeStruct((fine // 2 +...  5.25 us
    ppermute x1, starting transfers between devices, local(): tail = lax.ppermute(tail, 'tm', up)  3.96 us
    ppermute x1, waiting for transfers between devices, local(): ahead = lax.ppermute(own, both, around(1))  3.52 us
    pallas_call x2, Pallas kernels, correlate(): pl.pallas_call(functools.partial(correlate_kernel, scale=scale, first=fir...  3.07 us
  transfers between devices with their start and end apart: 5, of which 3 were waited for; matrix products, arithmetic and copies ran while one was open for 2% of the time, Pallas kernels for 10%

commit v1 on v0

--- a/solution.py
+++ b/solution.py
@@ -164,7 +164,7 @@
             split_low_ref[at, sub * lanes : (sub + 1) * lanes] = low
         return carry
 
-    lax.fori_loop(0, samples // 256, group, 0)
+    lax.fori_loop(0, samples // 256, group, 0, unroll=4)
     for step in range(samples // 1024):
         at = slice(step * 192, step * 192 + 192)
         high = split_high_ref[at, :]
@@ -231,7 +231,7 @@
                 split_low_ref[at, sub * lanes : (sub + 1) * lanes] = low
         return carry
 
-    lax.fori_loop(0, samples // 256, group, 0)
+    lax.fori_loop(0, samples // 256, group, 0, unroll=2)
     for step in range(samples // 1024):
         at = slice(step * 256, step * 256 + 256)
         high = split_high_ref[at, :]
@@ -523,7 +523,7 @@
     spectra = jnp.transpose(own.reshape(fine_dev, 2, blocks, own.shape[2]), (0, 2, 1, 3))
     later, spectra = lax.optimization_barrier((own, spectra))
     behind = lax.ppermute(later, both, around(-1))
-    first = fine_dev * 8 // 14
+    first = fine_dev * 10 // 14
     across_a = lax.ppermute(ahead[:first], both, around(1))
     across_b = lax.ppermute(ahead[first:], both, around(1))
     mine = (lax.axis_index("tm") * 128).astype(jnp.int32)[None]

time: 82.6 us -> 82 us (level)
    ppermute x1, waiting for transfers between devices: 1.68 us -> 0.2 us  [local(): across_b = lax.ppermute(ahead[first:], both, around(1))]
  transfers between devices with their start and end apart: 5 -> 5, of which waited for: 3 -> 3; matrix products, arithmetic and copies ran while one was open for 2% -> 2% of each run, Pallas kernels for 10% -> 11%
where the time goes in v1:
time: 82 us; the launch traced here: 81.4 us
  blocking collectives  37.3 us (45%)
  starting transfers between devices  18.4 us (22%)
  Pallas kernels  17.7 us (22%)
  waiting for transfers between devices  5.76 us (7%)
  local copies, waits for them, and re-layouts  1.55 us (2%)
    all_to_all x1, blocking collectives, local(): lax.all_to_all(sent.reshape(devices, fine_dev // 2, 2, lanes), 'chan', sp...  37.3 us
    pallas_call x1, Pallas kernels, own_part(): pl.pallas_call(own_kernel, out_shape=jax.ShapeDtypeStruct((fine + 256, 12...  5.97 us
    ppermute x1, starting transfers between devices, local(): across_a = lax.ppermute(ahead[:first], both, around(1))  5.32 us
    ppermute x1, starting transfers between devices, local(): ahead = lax.ppermute(own, both, around(1))  5.26 us
    pallas_call x1, Pallas kernels, tail_part(): pl.pallas_call(tail_kernel, out_shape=(jax.ShapeDtypeStruct((fine // 2 +...  5.13 us
    ppermute x1, starting transfers between devices, local(): tail = lax.ppermute(tail, 'tm', up)  3.96 us
    ppermute x1, waiting for transfers between devices, local(): ahead = lax.ppermute(own, both, around(1))  3.51 us
    pallas_call x2, Pallas kernels, correlate(): pl.pallas_call(functools.partial(correlate_kernel, scale=scale, first=fir...  3.06 us
  transfers between devices with their start and end apart: 5, of which 3 were waited for; matrix products, arithmetic and copies ran while one was open for 2% of the time, Pallas kernels for 11%

profile of v1, /device:TPU:1, one launch (start us, length us, event | category | flops | bytes accessed | tf_op | source)
XLA Modules:
  0.0 81.4 jit_solution(14672055099912440098)
XLA Ops:
  0.6 5.1 %tail_part.1 = (bf16[1344,128]{1,0:T(8,128)(2,1)}, f32[32,256]{1,0:T(8,128)}, s32[14]{0:T(128)}) custom-call(s32[224]{0:T(256)} %width_from.1, s32[224]{0:T(256)} %shift_from.1, bf16[4,16,7168]{2,1,0:T(8,128)(2,1)} %voltage_ref.3, f32[12,16]{1,0:T(8,128)} %taps_from.1), custom_call_target="tpu_custom_call" | custom-call | tf_op jit(solution)/shard_map/tail_part/pallas_call | solution.py:377
  5.8 4.0 %collective-permute-start = (bf16[1344,128]{1,0:T(8,128)(2,1)}, bf16[1344,128]{1,0:T(8,128)(2,1)S(1)}, u32[]{:S(2)}, u32[]{:S(2)}) collective-permute-start(bf16[1344,128]{1,0:T(8,128)(2,1)} %get-tuple-element.12), channel_id=1, source_target_pairs={{0,1},{1,2},{2,3},{4,5},{5,6},{6,7},{8,9},{9,10},{10,11},{12,13},{... | collective-permute-start | bytes 1032200 | tf_op jit(solution)/shard_map/ppermute | solution.py:502
  9.7 0.0 copy-start.1
  9.8 6.0 %own_part.1.window_ref = f32[2048,128]{1,0:T(8,128)} custom-call(s32[14]{0:T(128)} %get-tuple-element.9.base_from, bf16[4,16,7168]{2,1,0:T(8,128)(2,1)} %voltage_ref.3, f32[32,256]{1,0:T(8,128)} %get-tuple-element.10.rest_from), custom_call_target="tpu_custom_call" | custom-call | flops 5000000000 | bytes 4000000 | tf_op jit(solution)/shard_map/own_part/pallas_call | solution.py:406
  15.7 0.0 copy-done.1
  15.8 0.0 copy-start
  15.8 0.9 %place_part.1.place_ref = bf16[1792,1792]{1,0:T(8,128)(2,1)S(1)} custom-call(s32[1,1792]{1,0:T(1,128)S(1)} %broadcast_in_dim.6.slot_ref), custom_call_target="tpu_custom_call" | custom-call | flops 5000000000 | bytes 4000000 | tf_op jit(solution)/shard_map/place_part/pallas_call | solution.py:428
  16.7 0.0 collective-permute-done.tail_ref
  16.7 0.3 copy-done
  17.0 2.0 %send_part.1 = bf16[1792,128]{1,0:T(8,128)(2,1)S(1)} custom-call(f32[2048,128]{1,0:T(8,128)S(1)} %copy-done, bf16[1344,128]{1,0:T(8,128)(2,1)S(1)} %collective-permute-done.tail_ref, bf16[1792,1792]{1,0:T(8,128)(2,1)S(1)} %place_part.1.place_ref), custom_call_target="tpu_custom_call" | custom-call | tf_op jit(solution)/shard_map/send_part/pallas_call | solution.py:441
  19.0 37.3 %all_to_all.5 = bf16[128,7,2,128]{3,2,1,0:T(2,128)(2,1)S(1)} all-to-all(bf16[128,7,2,128]{3,2,1,0:T(2,128)(2,1)S(1)} %bitcast.9), channel_id=1, replica_groups=mesh['chan'=128,'tm'=4] {'chan'}, dimensions={0} | all-to-all | bytes 917504 | tf_op jit(solution)/shard_map/all_to_all | solution.py:508
  56.3 0.5 unpack.1.own_ref
  56.8 5.3 %collective-permute-start.1 = (bf16[14,32,512]{2,1,0:T(8,128)(2,1)S(1)}, bf16[14,32,512]{2,1,0:T(8,128)(2,1)S(1)}, u32[]{:S(2)}, u32[]{:S(2)}) collective-permute-start(bf16[14,32,512]{2,1,0:T(8,128)(2,1)S(1)} %unpack.1.own_ref), channel_id=1, source_target_pairs={{0,1},{1,2},{2,3},{3,0},{4,7},{5,4},{6,5},{7,6},{8,9},{9,10},{10,1... | collective-permute-start | bytes 1376264 | tf_op jit(solution)/shard_map/ppermute | solution.py:522
  62.1 1.2 %copy.10 = bf16[14,2,16,512]{3,1,2,0:T(2,128)(2,1)} copy(bf16[14,2,16,512]{3,2,1,0:T(8,128)(2,1)S(1)} %bitcast.7) | data formatting | bytes 917504 | tf_op jit(solution)/shard_map/reshape | solution.py:523
  63.4 1.9 %collective-permute-start.2 = (bf16[14,32,512]{2,1,0:T(8,128)(2,1)S(1)}, bf16[14,32,512]{2,1,0:T(8,128)(2,1)S(1)}, u32[]{:S(2)}, u32[]{:S(2)}) collective-permute-start(bf16[14,32,512]{2,1,0:T(8,128)(2,1)S(1)} %unpack.1.own_ref), channel_id=1, source_target_pairs={{0,3},{1,0},{2,1},{3,2},{4,5},{5,6},{6,7},{7,4},{8,11},{9,8},{10,9... | collective-permute-start | bytes 1376264 | tf_op jit(solution)/shard_map/ppermute | solution.py:525
  65.3 3.5 %collective-permute-done.1.ahead_ref = bf16[14,32,512]{2,1,0:T(8,128)(2,1)S(1)} collective-permute-done((bf16[14,32,512]{2,1,0:T(8,128)(2,1)S(1)}, bf16[14,32,512]{2,1,0:T(8,128)(2,1)S(1)}, u32[]{:S(2)}, u32[]{:S(2)}) %collective-permute-start.1) | collective-permute-done | bytes 458784 | tf_op jit(solution)/shard_map/ppermute | solution.py:522
  68.8 5.3 %collective-permute-start.4 = (bf16[10,32,512]{2,1,0:T(8,128)(2,1)S(1)}, bf16[10,32,512]{2,1,0:T(8,128)(2,1)S(1)}, u32[]{:S(2)}, u32[]{:S(2)}) collective-permute-start(bf16[10,32,512]{2,1,0:T(8,128)(2,1)S(1)} %slice.9), channel_id=1, source_target_pairs={{0,1},{1,2},{2,3},{3,0},{4,7},{5,4},{6,5},{7,6},{8,9},{9,10},{10,1... | collective-permute-start | bytes 983048 | tf_op jit(solution)/shard_map/ppermute | solution.py:527
  74.2 1.9 %collective-permute-start.3 = (bf16[4,32,512]{2,1,0:T(8,128)(2,1)S(1)}, bf16[4,32,512]{2,1,0:T(8,128)(2,1)S(1)}, u32[]{:S(2)}, u32[]{:S(2)}) collective-permute-start(bf16[4,32,512]{2,1,0:T(8,128)(2,1)S(1)} %slice.8), channel_id=1, source_target_pairs={{0,1},{1,2},{2,3},{3,0},{4,7},{5,4},{6,5},{7,6},{8,9},{9,10},{10,1... | collective-permute-start | bytes 393224 | tf_op jit(solution)/shard_map/ppermute | solution.py:528
  76.1 0.0 collective-permute-done.2.behind_ref
  76.1 2.0 %collective-permute-done.4.across_ref = bf16[10,32,512]{2,1,0:T(8,128)(2,1)S(1)} collective-permute-done((bf16[10,32,512]{2,1,0:T(8,128)(2,1)S(1)}, bf16[10,32,512]{2,1,0:T(8,128)(2,1)S(1)}, u32[]{:S(2)}, u32[]{:S(2)}) %collective-permute-start.4) | collective-permute-done | bytes 327712 | tf_op jit(solution)/shard_map/ppermute | solution.py:527
  78.1 1.8 %correlate.2.rest_0_ = bf16[14,2,128,512]{3,2,1,0:T(8,128)(2,1)} custom-call(s32[1]{0:T(128)} %bitcast.4.mine_ref, bf16[14,32,512]{2,1,0:T(8,128)(2,1)S(1)} %unpack.1.own_ref, bf16[14,32,512]{2,1,0:T(8,128)(2,1)S(1)} %collective-permute-done.1.ahead_ref, bf16[14,32,512]{2,1,0:T(8,128)(2,1)S(1)} %collective-permute-done.2.behind_ref, ...), custom_call_target="tpu_custom_call" | custom-call | flops 335544320 | bytes 4000000 | tf_op jit(solution)/shard_map/correlate/pallas_call | solution.py:474
  80.0 0.2 collective-permute-done.3.across_ref
  80.2 1.2 %correlate.3 = bf16[14,2,128,512]{3,2,1,0:T(8,128)(2,1)} custom-call(s32[1]{0:T(128)} %bitcast.4.mine_ref, bf16[14,32,512]{2,1,0:T(8,128)(2,1)S(1)} %unpack.1.own_ref, bf16[14,32,512]{2,1,0:T(8,128)(2,1)S(1)} %collective-permute-done.1.ahead_ref, bf16[14,32,512]{2,1,0:T(8,128)(2,1)S(1)} %collective-permute-done.2.behind_ref, ...), custom_call_target="tpu_custom_call", output_to_operand_aliasing={{}: (5, {})} | custom-call | flops 134217728 | bytes 4000000 | tf_op jit(solution)/shard_map/correlate/pallas_call | solution.py:474
  (3 shorter events, 0.0 us)
Async XLA Ops:
  5.8 10.9 %collective-permute-start = (bf16[1344,128]{1,0:T(8,128)(2,1)}, bf16[1344,128]{1,0:T(8,128)(2,1)S(1)}, u32[]{:S(2)}, u32[]{:S(2)}) collective-permute-start(bf16[1344,128]{1,0:T(8,128)(2,1)} %get-tuple-element.12), channel_id=1, source_target_pairs={{0,1},{1,2},{2,3},{4,5},{5,6},{6,7},{8,9},{9,10},{10,11},{12,13},{... | collective-permute-start | bytes 1032200 | tf_op jit(solution)/shard_map/ppermute | solution.py:502
  9.7 6.0 %copy-start.1 = (s32[1792]{0:T(1024)S(1)}, s32[1792]{0:T(1024)}, u32[]{:S(2)}) copy-start(s32[1792]{0:T(1024)} %param.9) | copy-start | bytes 21508
  15.8 1.2 %copy-start = (f32[2048,128]{1,0:T(8,128)S(1)}, f32[2048,128]{1,0:T(8,128)}, u32[]{:S(2)}) copy-start(f32[2048,128]{1,0:T(8,128)} %own_part.1.window_ref) | copy-start | bytes 3145732
  56.8 11.9 %collective-permute-start.1 = (bf16[14,32,512]{2,1,0:T(8,128)(2,1)S(1)}, bf16[14,32,512]{2,1,0:T(8,128)(2,1)S(1)}, u32[]{:S(2)}, u32[]{:S(2)}) collective-permute-start(bf16[14,32,512]{2,1,0:T(8,128)(2,1)S(1)} %unpack.1.own_ref), channel_id=1, source_target_pairs={{0,1},{1,2},{2,3},{3,0},{4,7},{5,4},{6,5},{7,6},{8,9},{9,10},{10,1... | collective-permute-start | bytes 1376264 | tf_op jit(solution)/shard_map/ppermute | solution.py:522
  63.4 12.7 %collective-permute-start.2 = (bf16[14,32,512]{2,1,0:T(8,128)(2,1)S(1)}, bf16[14,32,512]{2,1,0:T(8,128)(2,1)S(1)}, u32[]{:S(2)}, u32[]{:S(2)}) collective-permute-start(bf16[14,32,512]{2,1,0:T(8,128)(2,1)S(1)} %unpack.1.own_ref), channel_id=1, source_target_pairs={{0,3},{1,0},{2,1},{3,2},{4,5},{5,6},{6,7},{7,4},{8,11},{9,8},{10,9... | collective-permute-start | bytes 1376264 | tf_op jit(solution)/shard_map/ppermute | solution.py:525
  68.8 9.3 %collective-permute-start.4 = (bf16[10,32,512]{2,1,0:T(8,128)(2,1)S(1)}, bf16[10,32,512]{2,1,0:T(8,128)(2,1)S(1)}, u32[]{:S(2)}, u32[]{:S(2)}) collective-permute-start(bf16[10,32,512]{2,1,0:T(8,128)(2,1)S(1)} %slice.9), channel_id=1, source_target_pairs={{0,1},{1,2},{2,3},{3,0},{4,7},{5,4},{6,5},{7,6},{8,9},{9,10},{10,1... | collective-permute-start | bytes 983048 | tf_op jit(solution)/shard_map/ppermute | solution.py:527
  74.2 6.0 %collective-permute-start.3 = (bf16[4,32,512]{2,1,0:T(8,128)(2,1)S(1)}, bf16[4,32,512]{2,1,0:T(8,128)(2,1)S(1)}, u32[]{:S(2)}, u32[]{:S(2)}) collective-permute-start(bf16[4,32,512]{2,1,0:T(8,128)(2,1)S(1)} %slice.8), channel_id=1, source_target_pairs={{0,1},{1,2},{2,3},{3,0},{4,7},{5,4},{6,5},{7,6},{8,9},{9,10},{10,1... | collective-permute-start | bytes 393224 | tf_op jit(solution)/shard_map/ppermute | solution.py:528

commit v2 on v1

--- a/solution.py
+++ b/solution.py
@@ -79,6 +79,10 @@
         window_ref[pl.ds(pl.multiple_of(base + 16, 16), WIDE - 16), lanes] = picked[16:]
     else:
         window_ref[0:WIDE, lanes] = picked
+
+
+def late_rows(fine):
+    return (fine + 79) // 80 * 16
 
 
 def tail_kernel(
@@ -185,17 +189,24 @@
             preferred_element_type=F32,
         )
         store_windows(window_ref, bases[step], picked, step)
-    half, quarter = fine // 2, fine // 4
+    half, block = fine // 2, late_rows(fine)
     at = lax.broadcasted_iota(jnp.int32, (half, lanes), 1)
     out_ref[0:half, :] = jnp.where(
         at < 64, window_ref[0:half, :], pltpu.roll(window_ref[half:fine, :], 64, 1)
     ).astype(BF16)
-    at = lax.broadcasted_iota(jnp.int32, (quarter, lanes), 1)
-    packed = jnp.zeros((quarter, lanes), F32)
-    for j in range(4):
-        moved = pltpu.roll(window_ref[j * quarter : (j + 1) * quarter, :], (64 + j * 32) % lanes, 1)
-        packed = jnp.where(at // 32 == j, moved, packed)
-    out_ref[half : half + quarter, :] = packed.astype(BF16)
+    source = lax.broadcasted_iota(jnp.int32, (lanes, lanes), 0)
+    target = lax.broadcasted_iota(jnp.int32, (lanes, lanes), 1)
+    packed = jnp.zeros((block, lanes), F32)
+    for j in range(5):
+        part = window_ref[j * block : min((j + 1) * block, fine), :].astype(BF16)
+        if part.shape[0] < block:
+            part = jnp.concatenate([part, jnp.zeros((block - part.shape[0], lanes), BF16)], 0)
+        slot = target - 24 * j
+        chosen = (slot >= 0) & (slot < 24) & (source == 64 + (slot // 3) * 4 + slot % 3)
+        packed = packed + jnp.dot(
+            part, jnp.where(chosen, 1.0, 0.0).astype(BF16), preferred_element_type=F32
+        )
+    out_ref[half : half + block, :] = packed.astype(BF16)
 
 
 def own_kernel(
@@ -273,30 +284,27 @@
 
 def send_kernel(window_ref, tail_ref, place_ref, out_ref, bins_ref):
     fine, lanes = bins_ref.shape
-    half, quarter = fine // 2, fine // 4
+    half, block = fine // 2, late_rows(fine)
     source = lax.broadcasted_iota(jnp.int32, (lanes, lanes), 0)
     target = lax.broadcasted_iota(jnp.int32, (lanes, lanes), 1)
-    late = source - 64
-    early_lane = (source // 8) * 16 + source % 8
-    late_lane = (late // 4) * 16 + 8 + late % 4
-    spread = jnp.where(
-        ((source < 64) & (target == early_lane))
-        | ((source >= 64) & (source < 96) & (late % 4 < 3) & (target == late_lane)),
-        1.0,
-        0.0,
-    ).astype(BF16)
-    at = lax.broadcasted_iota(jnp.int32, (quarter, lanes), 1)
-    for j in range(4):
-        rows = slice((j % 2) * quarter, (j % 2 + 1) * quarter)
-        early = tail_ref[rows, :].astype(F32)
-        if j >= 2:
-            early = pltpu.roll(early, 64, 1)
-        late = tail_ref[half : half + quarter, :].astype(F32)
-        late = pltpu.roll(late, (64 - j * 32) % lanes, 1)
-        tail = jnp.where(at < 64, early, late).astype(BF16)
-        added = jnp.dot(tail, spread, preferred_element_type=F32)
-        rows = slice(j * quarter, (j + 1) * quarter)
-        bins_ref[rows, :] = (window_ref[rows, :] + added).astype(BF16)
+
+    def table(slot, size, per, first):
+        chosen = (slot >= 0) & (slot < size) & (target == (slot // per) * 16 + first + slot % per)
+        return jnp.where(chosen, 1.0, 0.0).astype(BF16)
+
+    early = [table(source - 64 * h, 64, 8, 0) for h in range(2)]
+    late = [table(source - 24 * j, 24, 3, 8) for j in range(5)]
+    cuts = sorted({0, half, fine} | {j * block for j in range(1, 5)})
+    for at, end in zip(cuts, cuts[1:]):
+        h, j = at // half, at // block
+        first = tail_ref[at - h * half : end - h * half, :]
+        second = tail_ref[half + at - j * block : half + end - j * block, :]
+        added = jnp.dot(
+            jnp.concatenate([first, second], 1),
+            jnp.concatenate([early[h], late[j]], 0),
+            preferred_element_type=F32,
+        )
+        bins_ref[at:end, :] = (window_ref[at:end, :] + added).astype(BF16)
     step_rows = 448
     for step in range(out_ref.shape[0] // step_rows):
         at = slice(step * step_rows, (step + 1) * step_rows)
@@ -377,7 +385,7 @@
     return pl.pallas_call(
         tail_kernel,
         out_shape=(
-            jax.ShapeDtypeStruct((fine // 2 + fine // 4, 128), BF16),
+            jax.ShapeDtypeStruct((fine // 2 + late_rows(fine), 128), BF16),
             jax.ShapeDtypeStruct((32, 256), F32),
             jax.ShapeDtypeStruct((samples // 512,), jnp.int32),
         ),

time: 82 us -> 81.9 us (level)
  no operation moved by 1% of the time
where the time goes in v2:
time: 81.9 us; the launch traced here: 81.3 us
  blocking collectives  36.9 us (45%)
  starting transfers between devices  18.3 us (22%)
  Pallas kernels  18 us (22%)
  waiting for transfers between devices  5.76 us (7%)
  local copies, waits for them, and re-layouts  1.55 us (2%)
    all_to_all x1, blocking collectives, local(): lax.all_to_all(sent.reshape(devices, fine_dev // 2, 2, lanes), 'chan', sp...  36.9 us
    pallas_call x1, Pallas kernels, own_part(): pl.pallas_call(own_kernel, out_shape=jax.ShapeDtypeStruct((fine + 256, 12...  5.97 us
    pallas_call x1, Pallas kernels, tail_part(): pl.pallas_call(tail_kernel, out_shape=(jax.ShapeDtypeStruct((fine // 2 +...  5.4 us
    ppermute x1, starting transfers between devices, local(): across_a = lax.ppermute(ahead[:first], both, around(1))  5.32 us
    ppermute x1, starting transfers between devices, local(): ahead = lax.ppermute(own, both, around(1))  5.19 us
    ppermute x1, starting transfers between devices, local(): tail = lax.ppermute(tail, 'tm', up)  3.96 us
    ppermute x1, waiting for transfers between devices, local(): ahead = lax.ppermute(own, both, around(1))  3.51 us
    pallas_call x2, Pallas kernels, correlate(): pl.pallas_call(functools.partial(correlate_kernel, scale=scale, first=fir...  3.06 us
  transfers between devices with their start and end apart: 5, of which 3 were waited for; matrix products, arithmetic and copies ran while one was open for 2% of the time, Pallas kernels for 11%

profile of v2, /device:TPU:1, one launch (start us, length us, event | category | flops | bytes accessed | tf_op | source)
XLA Modules:
  0.0 81.3 jit_solution(10521352623370202860)
XLA Ops:
  0.6 5.4 %tail_part.1 = (bf16[1264,128]{1,0:T(8,128)(2,1)}, f32[32,256]{1,0:T(8,128)}, s32[14]{0:T(128)}) custom-call(s32[224]{0:T(256)} %width_from.1, s32[224]{0:T(256)} %shift_from.1, bf16[4,16,7168]{2,1,0:T(8,128)(2,1)} %voltage_ref.3, f32[12,16]{1,0:T(8,128)} %taps_from.1), custom_call_target="tpu_custom_call" | custom-call | tf_op jit(solution)/shard_map/tail_part/pallas_call | solution.py:385
  6.0 4.0 %collective-permute-start = (bf16[1264,128]{1,0:T(8,128)(2,1)}, bf16[1264,128]{1,0:T(8,128)(2,1)S(1)}, u32[]{:S(2)}, u32[]{:S(2)}) collective-permute-start(bf16[1264,128]{1,0:T(8,128)(2,1)} %get-tuple-element.12), channel_id=1, source_target_pairs={{0,1},{1,2},{2,3},{4,5},{5,6},{6,7},{8,9},{9,10},{10,11},{12,13},{... | collective-permute-start | bytes 970760 | tf_op jit(solution)/shard_map/ppermute | solution.py:510
  10.0 0.0 copy-start.1
  10.0 6.0 %own_part.1.window_ref = f32[2048,128]{1,0:T(8,128)} custom-call(s32[14]{0:T(128)} %get-tuple-element.9.base_from, bf16[4,16,7168]{2,1,0:T(8,128)(2,1)} %voltage_ref.3, f32[32,256]{1,0:T(8,128)} %get-tuple-element.10.rest_from), custom_call_target="tpu_custom_call" | custom-call | flops 5000000000 | bytes 4000000 | tf_op jit(solution)/shard_map/own_part/pallas_call | solution.py:414
  16.0 0.0 copy-done.1
  16.0 0.0 copy-start
  16.0 0.9 %place_part.1.place_ref = bf16[1792,1792]{1,0:T(8,128)(2,1)S(1)} custom-call(s32[1,1792]{1,0:T(1,128)S(1)} %broadcast_in_dim.6.slot_ref), custom_call_target="tpu_custom_call" | custom-call | flops 5000000000 | bytes 4000000 | tf_op jit(solution)/shard_map/place_part/pallas_call | solution.py:436
  17.0 0.0 collective-permute-done.tail_ref
  17.0 0.3 copy-done
  17.3 2.1 %send_part.1 = bf16[1792,128]{1,0:T(8,128)(2,1)S(1)} custom-call(f32[2048,128]{1,0:T(8,128)S(1)} %copy-done, bf16[1264,128]{1,0:T(8,128)(2,1)S(1)} %collective-permute-done.tail_ref, bf16[1792,1792]{1,0:T(8,128)(2,1)S(1)} %place_part.1.place_ref), custom_call_target="tpu_custom_call" | custom-call | tf_op jit(solution)/shard_map/send_part/pallas_call | solution.py:449
  19.3 36.9 %all_to_all.5 = bf16[128,7,2,128]{3,2,1,0:T(2,128)(2,1)S(1)} all-to-all(bf16[128,7,2,128]{3,2,1,0:T(2,128)(2,1)S(1)} %bitcast.9), channel_id=1, replica_groups=mesh['chan'=128,'tm'=4] {'chan'}, dimensions={0} | all-to-all | bytes 917504 | tf_op jit(solution)/shard_map/all_to_all | solution.py:516
  56.3 0.5 unpack.1.own_ref
  56.8 5.2 %collective-permute-start.1 = (bf16[14,32,512]{2,1,0:T(8,128)(2,1)S(1)}, bf16[14,32,512]{2,1,0:T(8,128)(2,1)S(1)}, u32[]{:S(2)}, u32[]{:S(2)}) collective-permute-start(bf16[14,32,512]{2,1,0:T(8,128)(2,1)S(1)} %unpack.1.own_ref), channel_id=1, source_target_pairs={{0,1},{1,2},{2,3},{3,0},{4,7},{5,4},{6,5},{7,6},{8,9},{9,10},{10,1... | collective-permute-start | bytes 1376264 | tf_op jit(solution)/shard_map/ppermute | solution.py:530
  62.0 1.2 %copy.10 = bf16[14,2,16,512]{3,1,2,0:T(2,128)(2,1)} copy(bf16[14,2,16,512]{3,2,1,0:T(8,128)(2,1)S(1)} %bitcast.7) | data formatting | bytes 917504 | tf_op jit(solution)/shard_map/reshape | solution.py:531
  63.2 1.9 %collective-permute-start.2 = (bf16[14,32,512]{2,1,0:T(8,128)(2,1)S(1)}, bf16[14,32,512]{2,1,0:T(8,128)(2,1)S(1)}, u32[]{:S(2)}, u32[]{:S(2)}) collective-permute-start(bf16[14,32,512]{2,1,0:T(8,128)(2,1)S(1)} %unpack.1.own_ref), channel_id=1, source_target_pairs={{0,3},{1,0},{2,1},{3,2},{4,5},{5,6},{6,7},{7,4},{8,11},{9,8},{10,9... | collective-permute-start | bytes 1376264 | tf_op jit(solution)/shard_map/ppermute | solution.py:533
  65.1 3.5 %collective-permute-done.1.ahead_ref = bf16[14,32,512]{2,1,0:T(8,128)(2,1)S(1)} collective-permute-done((bf16[14,32,512]{2,1,0:T(8,128)(2,1)S(1)}, bf16[14,32,512]{2,1,0:T(8,128)(2,1)S(1)}, u32[]{:S(2)}, u32[]{:S(2)}) %collective-permute-start.1) | collective-permute-done | bytes 458784 | tf_op jit(solution)/shard_map/ppermute | solution.py:530
  68.7 5.3 %collective-permute-start.4 = (bf16[10,32,512]{2,1,0:T(8,128)(2,1)S(1)}, bf16[10,32,512]{2,1,0:T(8,128)(2,1)S(1)}, u32[]{:S(2)}, u32[]{:S(2)}) collective-permute-start(bf16[10,32,512]{2,1,0:T(8,128)(2,1)S(1)} %slice.9), channel_id=1, source_target_pairs={{0,1},{1,2},{2,3},{3,0},{4,7},{5,4},{6,5},{7,6},{8,9},{9,10},{10,1... | collective-permute-start | bytes 983048 | tf_op jit(solution)/shard_map/ppermute | solution.py:535
  74.0 1.9 %collective-permute-start.3 = (bf16[4,32,512]{2,1,0:T(8,128)(2,1)S(1)}, bf16[4,32,512]{2,1,0:T(8,128)(2,1)S(1)}, u32[]{:S(2)}, u32[]{:S(2)}) collective-permute-start(bf16[4,32,512]{2,1,0:T(8,128)(2,1)S(1)} %slice.8), channel_id=1, source_target_pairs={{0,1},{1,2},{2,3},{3,0},{4,7},{5,4},{6,5},{7,6},{8,9},{9,10},{10,1... | collective-permute-start | bytes 393224 | tf_op jit(solution)/shard_map/ppermute | solution.py:536
  76.0 0.0 collective-permute-done.2.behind_ref
  76.0 2.0 %collective-permute-done.4.across_ref = bf16[10,32,512]{2,1,0:T(8,128)(2,1)S(1)} collective-permute-done((bf16[10,32,512]{2,1,0:T(8,128)(2,1)S(1)}, bf16[10,32,512]{2,1,0:T(8,128)(2,1)S(1)}, u32[]{:S(2)}, u32[]{:S(2)}) %collective-permute-start.4) | collective-permute-done | bytes 327712 | tf_op jit(solution)/shard_map/ppermute | solution.py:535
  78.0 1.8 %correlate.2.rest_0_ = bf16[14,2,128,512]{3,2,1,0:T(8,128)(2,1)} custom-call(s32[1]{0:T(128)} %bitcast.4.mine_ref, bf16[14,32,512]{2,1,0:T(8,128)(2,1)S(1)} %unpack.1.own_ref, bf16[14,32,512]{2,1,0:T(8,128)(2,1)S(1)} %collective-permute-done.1.ahead_ref, bf16[14,32,512]{2,1,0:T(8,128)(2,1)S(1)} %collective-permute-done.2.behind_ref, ...), custom_call_target="tpu_custom_call" | custom-call | flops 335544320 | bytes 4000000 | tf_op jit(solution)/shard_map/correlate/pallas_call | solution.py:482
  79.8 0.2 collective-permute-done.3.across_ref
  80.0 1.2 %correlate.3 = bf16[14,2,128,512]{3,2,1,0:T(8,128)(2,1)} custom-call(s32[1]{0:T(128)} %bitcast.4.mine_ref, bf16[14,32,512]{2,1,0:T(8,128)(2,1)S(1)} %unpack.1.own_ref, bf16[14,32,512]{2,1,0:T(8,128)(2,1)S(1)} %collective-permute-done.1.ahead_ref, bf16[14,32,512]{2,1,0:T(8,128)(2,1)S(1)} %collective-permute-done.2.behind_ref, ...), custom_call_target="tpu_custom_call", output_to_operand_aliasing={{}: (5, {})} | custom-call | flops 134217728 | bytes 4000000 | tf_op jit(solution)/shard_map/correlate/pallas_call | solution.py:482
  (3 shorter events, 0.0 us)
Async XLA Ops:
  6.0 10.9 %collective-permute-start = (bf16[1264,128]{1,0:T(8,128)(2,1)}, bf16[1264,128]{1,0:T(8,128)(2,1)S(1)}, u32[]{:S(2)}, u32[]{:S(2)}) collective-permute-start(bf16[1264,128]{1,0:T(8,128)(2,1)} %get-tuple-element.12), channel_id=1, source_target_pairs={{0,1},{1,2},{2,3},{4,5},{5,6},{6,7},{8,9},{9,10},{10,11},{12,13},{... | collective-permute-start | bytes 970760 | tf_op jit(solution)/shard_map/ppermute | solution.py:510
  10.0 6.0 %copy-start.1 = (s32[1792]{0:T(1024)S(1)}, s32[1792]{0:T(1024)}, u32[]{:S(2)}) copy-start(s32[1792]{0:T(1024)} %param.9) | copy-start | bytes 21508
  16.0 1.2 %copy-start = (f32[2048,128]{1,0:T(8,128)S(1)}, f32[2048,128]{1,0:T(8,128)}, u32[]{:S(2)}) copy-start(f32[2048,128]{1,0:T(8,128)} %own_part.1.window_ref) | copy-start | bytes 3145732
  56.8 11.9 %collective-permute-start.1 = (bf16[14,32,512]{2,1,0:T(8,128)(2,1)S(1)}, bf16[14,32,512]{2,1,0:T(8,128)(2,1)S(1)}, u32[]{:S(2)}, u32[]{:S(2)}) collective-permute-start(bf16[14,32,512]{2,1,0:T(8,128)(2,1)S(1)} %unpack.1.own_ref), channel_id=1, source_target_pairs={{0,1},{1,2},{2,3},{3,0},{4,7},{5,4},{6,5},{7,6},{8,9},{9,10},{10,1... | collective-permute-start | bytes 1376264 | tf_op jit(solution)/shard_map/ppermute | solution.py:530
  63.2 12.7 %collective-permute-start.2 = (bf16[14,32,512]{2,1,0:T(8,128)(2,1)S(1)}, bf16[14,32,512]{2,1,0:T(8,128)(2,1)S(1)}, u32[]{:S(2)}, u32[]{:S(2)}) collective-permute-start(bf16[14,32,512]{2,1,0:T(8,128)(2,1)S(1)} %unpack.1.own_ref), channel_id=1, source_target_pairs={{0,3},{1,0},{2,1},{3,2},{4,5},{5,6},{6,7},{7,4},{8,11},{9,8},{10,9... | collective-permute-start | bytes 1376264 | tf_op jit(solution)/shard_map/ppermute | solution.py:533
  68.7 9.3 %collective-permute-start.4 = (bf16[10,32,512]{2,1,0:T(8,128)(2,1)S(1)}, bf16[10,32,512]{2,1,0:T(8,128)(2,1)S(1)}, u32[]{:S(2)}, u32[]{:S(2)}) collective-permute-start(bf16[10,32,512]{2,1,0:T(8,128)(2,1)S(1)} %slice.9), channel_id=1, source_target_pairs={{0,1},{1,2},{2,3},{3,0},{4,7},{5,4},{6,5},{7,6},{8,9},{9,10},{10,1... | collective-permute-start | bytes 983048 | tf_op jit(solution)/shard_map/ppermute | solution.py:535
  74.0 6.0 %collective-permute-start.3 = (bf16[4,32,512]{2,1,0:T(8,128)(2,1)S(1)}, bf16[4,32,512]{2,1,0:T(8,128)(2,1)S(1)}, u32[]{:S(2)}, u32[]{:S(2)}) collective-permute-start(bf16[4,32,512]{2,1,0:T(8,128)(2,1)S(1)} %slice.8), channel_id=1, source_target_pairs={{0,1},{1,2},{2,3},{3,0},{4,7},{5,4},{6,5},{7,6},{8,9},{9,10},{10,1... | collective-permute-start | bytes 393224 | tf_op jit(solution)/shard_map/ppermute | solution.py:536
